TPU v7x, 512 devices: a whole 4x8x8 slice. The times are simulated.
512 devices in a mesh: bulk: 32 (over x, y), slide: 16 (over z, core).
Axes of the slice: x: 4, y: 8, z: 8, core: 2. Of those that a mesh axis runs over, the one named last changes fastest.
Arguments:
- tile_images: bfloat16 [16, 2048, 8, 8, 192], P('slide', 'bulk'), may hold values from -6 to 6
- destination: int32 [16, 2048], P('slide', 'bulk'), may hold values from -1 to 31, as said below
- encoder_slot: int32 [16, 2048], P('slide', 'bulk'), may hold values from -1 to 23, as said below
- tile_slide: int32 [16, 2048], P('slide', 'bulk'), may hold values from -1 to 3, as said below
- slide_tiles: int32 [16, 128], P('slide', 'bulk'), may hold values from 1 to 61, as said below
- targets: float32 [16, 128, 256], P('slide', 'bulk'), may hold values from -6 to 6
- depth_taps: float32 [49, 192], replicated, may hold values from -0.875 to 0.875
- first_proj: bfloat16 [192, 768], replicated, may hold values from -0.4375 to 0.4375
- second_proj: bfloat16 [768, 192], replicated, may hold values from -0.21875 to 0.21875
- reduce_proj: bfloat16 [768, 384], replicated, may hold values from -0.21875 to 0.21875
- head_proj: float32 [384, 256], replicated, may hold values from -0.3125 to 0.3125
Outputs:
- predictions: float32 [16, 128, 256], P('slide', 'bulk')
- embedding_cache: float32 [16, 768, 384], P('slide', 'bulk')
- grad_taps: float32 [49, 192], replicated
- grad_first: float32 [192, 768], replicated
- grad_second: float32 [768, 192], replicated
- grad_reduce: float32 [768, 384], replicated
Inputs may be any that keep to these rules, and one draw needn't show every extreme that they name: `destination`: -1 marks an empty slot. In each replica every encoder index receives exactly 24 live tiles, at most 2 from the slots of one owner; in each replica some owner has all 64 slots live and sends exactly 2 to every encoder. `encoder_slot`: -1 exactly on empty slots; the 24 live tiles of one encoder in one replica carry the slot numbers 0 to 23 once each. `tile_slide`: -1 exactly on empty slots; every slide of every owner has one or more live tiles. `slide_tiles`: the number of live tiles of each slide; in each replica some slide has 61 of them.
All inputs are finite; a program needn't handle non-finite values.
Results may differ from a plain program's by a relative error of at most 0.006.
Values may be sent and summed in bfloat16 or wider, within the bound.
A program may use at most 128 MiB of HBM per device.

v0:
```python
import jax
import jax.numpy as jnp
from jax import lax
from jax.sharding import PartitionSpec as P

KSIZE = 7


norm_eps = 1e-06
root_half = 0.7071067811865476
normal_peak = 0.3989422804014327


def norm_rows(values):
    centered = values - jnp.mean(values, axis=-1, keepdims=True)
    factor = lax.rsqrt(jnp.mean(centered * centered, axis=-1, keepdims=True) + norm_eps)
    return (centered * factor, factor)


def norm_back(normed, factor, incoming):
    return factor * (
        incoming
        - jnp.mean(incoming, axis=-1, keepdims=True)
        - normed * jnp.mean(incoming * normed, axis=-1, keepdims=True)
    )


def gelu_exact(values):
    return 0.5 * values * (1.0 + lax.erf(values * root_half))


def gelu_slope(values):
    return (
        0.5 * (1.0 + lax.erf(values * root_half))
        + values * jnp.exp(-0.5 * values * values) * normal_peak
    )


def padded_float(images):
    margin = KSIZE // 2
    return jnp.pad(images.astype(jnp.float32), ((0, 0), (margin, margin), (margin, margin), (0, 0)))


def depthwise(padded, taps, side):
    total = jnp.zeros((padded.shape[0], side, side, padded.shape[3]), jnp.float32)
    for vertical in range(KSIZE):
        for lateral in range(KSIZE):
            total = (
                total
                + padded[:, vertical : vertical + side, lateral : lateral + side, :]
                * taps[vertical * KSIZE + lateral]
            )
    return total


def encode(images, taps, first_proj, second_proj, reduce_proj):
    count, side, _, chans = images.shape
    flat_rows = count * side * side
    inputs = images.astype(jnp.float32)
    spatial = depthwise(padded_float(images), taps, side)
    normed, first_factor = norm_rows(spatial)
    normed_low = normed.astype(jnp.bfloat16)
    hidden = jnp.dot(
        normed_low.reshape(flat_rows, chans), first_proj, preferred_element_type=jnp.float32
    )
    active = gelu_exact(hidden).astype(jnp.bfloat16)
    branch = jnp.dot(active, second_proj, preferred_element_type=jnp.float32)
    summed = inputs + branch.reshape(inputs.shape)
    second_normed, second_factor = norm_rows(summed)
    patches = lax.optimization_barrier(second_normed.astype(jnp.bfloat16)).astype(jnp.float32)
    blocks = patches.reshape(count, side // 2, 2, side // 2, 2, chans)
    pooled_patch = jnp.mean(blocks, axis=(1, 3)).reshape(count, 4 * chans)
    reduced = jnp.dot(
        pooled_patch, reduce_proj.astype(jnp.float32), precision=lax.Precision.HIGHEST
    )
    embedded, third_factor = norm_rows(reduced)
    hidden_rows = hidden.reshape(count, side * side, hidden.shape[1])
    active_rows = active.reshape(count, side * side, active.shape[1])
    saved = (
        normed,
        first_factor,
        normed_low,
        hidden_rows,
        active_rows,
        second_normed,
        second_factor,
        pooled_patch,
        embedded,
        third_factor,
    )
    return (embedded, saved)


def gradients(images, saved, cotangent, first_proj, second_proj, reduce_proj):
    (
        normed,
        first_factor,
        normed_low,
        hidden_rows,
        active_rows,
        second_normed,
        second_factor,
        pooled_patch,
        embedded,
        third_factor,
    ) = saved
    count, side, _, chans = images.shape
    flat_rows = count * side * side
    back_reduced = norm_back(embedded, third_factor, cotangent)
    grad_reduce = jnp.dot(pooled_patch.T, back_reduced, precision=lax.Precision.HIGHEST)
    back_patch = jnp.dot(
        back_reduced, reduce_proj.astype(jnp.float32).T, precision=lax.Precision.HIGHEST
    ) / (side // 2 * (side // 2))
    back_blocks = jnp.broadcast_to(
        back_patch.reshape(count, 1, 2, 1, 2, chans), (count, side // 2, 2, side // 2, 2, chans)
    ).reshape(count, side, side, chans)
    back_summed = norm_back(second_normed, second_factor, back_blocks)
    summed_low = back_summed.reshape(flat_rows, chans).astype(jnp.bfloat16)
    active = active_rows.reshape(flat_rows, active_rows.shape[2])
    hidden = hidden_rows.reshape(flat_rows, hidden_rows.shape[2])
    grad_second = jnp.dot(active.T, summed_low, preferred_element_type=jnp.float32)
    back_hidden = jnp.dot(
        summed_low, second_proj.T, preferred_element_type=jnp.float32
    ) * gelu_slope(hidden)
    hidden_low = back_hidden.astype(jnp.bfloat16)
    grad_first = jnp.dot(
        normed_low.reshape(flat_rows, chans).T, hidden_low, preferred_element_type=jnp.float32
    )
    back_normed = jnp.dot(hidden_low, first_proj.T, preferred_element_type=jnp.float32).reshape(
        count, side, side, chans
    )
    back_spatial = norm_back(normed, first_factor, back_normed)
    padded = padded_float(images)
    tap_list = []
    for vertical in range(KSIZE):
        for lateral in range(KSIZE):
            window = padded[:, vertical : vertical + side, lateral : lateral + side, :]
            tap_list.append(jnp.sum(window * back_spatial, axis=(0, 1, 2)))
    grad_taps = jnp.stack(tap_list, axis=0)
    return (grad_taps, grad_first, grad_second, grad_reduce)


def blocked_gradients(
    images, saved, cotangent, first_proj, second_proj, reduce_proj, unit_rows, taps_shape
):
    groups = images.shape[0] // unit_rows

    def split_rows(array):
        return array.reshape((groups, unit_rows) + array.shape[1:])

    def advance(carry, pieces):
        piece_images, piece_saved, piece_back = pieces
        found = gradients(
            piece_images, piece_saved, piece_back, first_proj, second_proj, reduce_proj
        )
        return (tuple((first + second for first, second in zip(carry, found))), None)

    start = (
        jnp.zeros(taps_shape, jnp.float32),
        jnp.zeros(first_proj.shape, jnp.float32),
        jnp.zeros(second_proj.shape, jnp.float32),
        jnp.zeros(reduce_proj.shape, jnp.float32),
    )
    totals, _ = lax.scan(
        advance, start, (split_rows(images), jax.tree.map(split_rows, saved), split_rows(cotangent))
    )
    return totals


def local(
    tile_images,
    destination,
    encoder_slot,
    tile_slide,
    slide_tiles,
    targets,
    depth_taps,
    first_proj,
    second_proj,
    reduce_proj,
    head_proj,
):
    bulk_count = lax.axis_size("bulk")
    capacity = tile_images.shape[1]
    per_peer = capacity // bulk_count
    encoder_rows = 3 * capacity // 8
    unit_rows = capacity // 8
    owned = tile_images[0]
    dests = destination[0]
    slot_numbers = encoder_slot[0]
    slides = tile_slide[0]
    slide_count = slide_tiles.shape[1]
    slots_range = jnp.arange(capacity, dtype=jnp.int32)
    live = dests >= 0
    earlier = (
        (dests[None, :] == dests[:, None])
        & live[None, :]
        & (slots_range[None, :] < slots_range[:, None])
    )
    rank_here = jnp.sum(earlier.astype(jnp.int32), axis=1)
    position = jnp.where(live, dests * per_peer + rank_here, -1)
    matches = position[None, :] == slots_range[:, None]
    filled = jnp.any(matches, axis=1)
    source = jnp.sum(jnp.where(matches, slots_range[None, :], 0), axis=1)
    outgoing_slots = jnp.where(filled, slot_numbers[source], -1)
    incoming_slots = lax.all_to_all(outgoing_slots, "bulk", split_axis=0, concat_axis=0, tiled=True)
    encoder_range = jnp.arange(encoder_rows, dtype=jnp.int32)
    pick = jnp.sum(
        jnp.where(incoming_slots[None, :] == encoder_range[:, None], slots_range[None, :], 0),
        axis=1,
    )
    member = (slides[None, :] == jnp.arange(slide_count, dtype=jnp.int32)[:, None]).astype(
        jnp.float32
    )
    counts = slide_tiles[0].astype(jnp.float32)[:, None]
    embedded, saved = encode(owned, depth_taps, first_proj, second_proj, reduce_proj)
    embedded_own = jnp.where(live[:, None], embedded, 0.0)
    sending = jnp.where(filled[:, None], embedded_own[source], 0.0)
    received = lax.all_to_all(sending, "bulk", split_axis=0, concat_axis=0, tiled=True)
    cache_rows = received[pick]
    pooled = jnp.dot(member, embedded_own, precision=lax.Precision.HIGHEST) / counts
    predicted = jnp.dot(pooled, head_proj, precision=lax.Precision.HIGHEST)
    back_pooled = (
        jnp.dot(predicted - targets[0], head_proj.T, precision=lax.Precision.HIGHEST) / counts
    )
    predicted, back_own = (
        predicted,
        jnp.dot(member.T, back_pooled, precision=lax.Precision.HIGHEST),
    )
    found = blocked_gradients(
        owned, saved, back_own, first_proj, second_proj, reduce_proj, unit_rows, depth_taps.shape
    )
    grad_taps, grad_first, grad_second, grad_reduce = lax.psum(
        (found[0], found[1], found[2], found[3]), ("bulk", "slide")
    )
    return (predicted[None], cache_rows[None], grad_taps, grad_first, grad_second, grad_reduce)


def solution(mesh):
    in_specs = (
        P("slide", "bulk", None, None, None),
        P("slide", "bulk"),
        P("slide", "bulk"),
        P("slide", "bulk"),
        P("slide", "bulk"),
        P("slide", "bulk", None),
        P(),
        P(),
        P(),
        P(),
        P(),
    )
    out_specs = (P("slide", "bulk", None), P("slide", "bulk", None), P(), P(), P(), P())
    return jax.shard_map(local, mesh=mesh, in_specs=in_specs, out_specs=out_specs, check_vma=False)
```

profile of v0, /device:TPU:1, one launch (start us, length us, event | category | flops | bytes accessed | tf_op | source)
XLA Modules:
  0.0 691.9 jit_solution(3452242008380674801)
XLA Ops:
  10.3 4.1 convert_bitcast_fusion
  14.3 81.2 %fusion.241 = (f32[64,8,8]{2,1,0:T(8,128)S(1)}, f32[64,8,8,192]{3,2,1,0:T(8,128)S(1)}) fusion(f32[192]{0:T(256)S(1)} %bitcast.501, f32[192]{0:T(256)S(1)} %bitcast.502, f32[192]{0:T(256)S(1)} %bitcast.474, f32[192]{0:T(256)S(1)} %bitcast.475, f32[192]{0:T(256)S(1)} %bitcast.476, f32[192]{0:T(256)S(1)} %bitcast.477, f32[192]{0:T(256)S(1)} %bitcast.478, ...), kind=kLoop, calls=%fused_computation.409 | loop fusion | flops 77066240 | bytes 6345472 | tf_op jit(solution)/shard_map/reduce_sum | solution.py:15
  97.0 3.1 fusion.240
  100.1 4.9 copy.60
  105.0 6.4 multiply_convert_fusion.1
  111.4 3.9 fusion.239
  117.5 2.2 multiply_reduce_fusion.4
  125.1 3.3 copy.59
  128.4 3.6 multiply_convert_fusion.2
  132.0 3.7 reshape.581
  135.7 4.6 reduce_sum.750
  147.6 4.8 subtract_multiply_fusion
  152.5 239.3 %while.19 = (s32[]{:T(128)}, f32[49,192]{1,0:T(8,128)S(1)}, f32[192,768]{1,0:T(8,128)}, f32[768,192]{0,1:T(8,128)}, f32[768,384]{1,0:T(8,128)}, /*index=5*/bf16[...) while((s32[]{:T(128)}, f32[49,192]{1,0:T(8,128)S(1)}, ...), condition=%wide.region_67.68_spmd.clone, body=%wide.region_11.67_spmd.clone.sunk | while | flops 677468352 | bytes 39302580 | solution.py:164
  161.4 1.7 fusion.303
  177.3 2.3 convolution_add_fusion.8
  189.5 1.7 fusion.303
  202.0 2.3 convolution_add_fusion.7
  205.2 2.2 convolution_add_fusion.6
  207.4 2.3 convolution_add_fusion.8
  219.7 1.7 fusion.303
  232.2 2.3 convolution_add_fusion.7
  235.4 2.2 convolution_add_fusion.6
  237.7 2.3 convolution_add_fusion.8
  249.9 1.7 fusion.303
  262.3 2.3 convolution_add_fusion.7
  265.6 2.2 convolution_add_fusion.6
  267.8 2.3 convolution_add_fusion.8
  280.0 1.7 fusion.303
  292.5 2.3 convolution_add_fusion.7
  295.7 2.2 convolution_add_fusion.6
  298.0 2.3 convolution_add_fusion.8
  322.7 2.3 convolution_add_fusion.7
  325.9 2.2 convolution_add_fusion.6
  328.1 2.3 convolution_add_fusion.8
  352.8 2.3 convolution_add_fusion.7
  356.1 2.2 convolution_add_fusion.6
  358.3 2.3 convolution_add_fusion.8
  383.0 2.3 convolution_add_fusion.7
  386.2 2.2 convolution_add_fusion.6
  388.5 2.3 convolution_add_fusion.8
  395.9 10.5 %all-to-all-start.1 = ((s32[32,2,1]{1,2,0:T(1,128)}), s32[32,2,1]{1,2,0:T(1,128)S(1)}, u32[]{:S(2)}, u32[]{:S(2)}) async-start(s32[32,2,1]{1,2,0:T(1,128)} %bitcast.63), calls=%async_computation.1 | async-start | bytes 32768 | tf_op jit(solution)/shard_map/all_to_all | solution.py:206
  408.9 106.0 %psum.28 = f32[49,192]{1,0:T(8,128)} all-reduce(f32[49,192]{1,0:T(8,128)S(1)} %get-tuple-element.254), channel_id=1, replica_groups=mesh['bulk'=32,'slide'=16] {'bulk','slide'}, use_global_device_ids=true, to_apply=%region_68.69 | all-reduce | flops 9408 | bytes 75264 | tf_op jit(solution)/shard_map/psum | solution.py:233
  514.9 6.2 all-to-all-start
  522.6 7.6 %all-to-all-done = f32[32,2,384]{2,1,0:T(2,128)S(1)} async-done(((f32[32,2,384]{2,1,0:T(2,128)}), f32[32,2,384]{2,1,0:T(2,128)S(1)}, u32[]{:S(2)}, u32[]{:S(2)}) %all-to-all-start) | async-done | bytes 98336 | tf_op jit(solution)/shard_map/all_to_all | solution.py:219
  531.4 147.5 %all-reduce.5.cloned.1.call-done = (f32[192,768]{1,0:T(8,128)}, f32[768,192]{0,1:T(8,128)}, f32[768,384]{1,0:T(8,128)}) async-done(((f32[192,768]{1,0:T(8,128)}, f32[768,192]{0,1:T(8,128)}, f32[768,384]{1,0:T(8,128)}), (f32[192,768]{1,0:T(8,128)}, f32[768,192]{0,1:T(8,128)}, f32[768,384]{1,0:T(8,128)})) %all-reduce.5.cloned.1.call-update) | async-done | bytes 2359312 | tf_op jit(solution)/shard_map/psum | solution.py:233
  678.9 1.9 copy.97
  680.8 1.9 copy.98
  682.7 2.4 copy.99
  (516 shorter events, 207.6 us)
Async XLA Ops:
  7.2 138.8 %copy-start = (f32[384,256]{1,0:T(8,128)S(1)}, f32[384,256]{1,0:T(8,128)}, u32[]{:S(2)}) copy-start(f32[384,256]{1,0:T(8,128)} %param.23) | copy-start | bytes 1179652
  7.2 671.7 %all-reduce.5.cloned.1.call-start = ((), (), s32[]{:S(2)}) async-start(), calls=%async_computation.2 | async-start | bytes 4718592 | tf_op jit(solution)/shard_map/psum | solution.py:233
  97.0 3.1 copy-start.11
  100.1 11.2 %copy-start.7 = (bf16[64,8,8,192]{3,2,1,0:T(8,128)(2,1)}, bf16[64,8,8,192]{3,2,1,0:T(8,128)(2,1)S(1)}, u32[]{:S(2)}) copy-start(bf16[64,8,8,192]{3,2,1,0:T(8,128)(2,1)S(1)} %get-tuple-element.520) | copy-start | bytes 4718596
  100.1 4.9 copy-start.8
  105.0 6.4 copy-start.6
  105.0 6.4 copy-start.14
  111.4 3.9 copy-start.3
  135.7 6.0 copy-start.15
  135.7 8.7 %copy-start.21 = (s32[1,64]{1,0:T(1,128)S(1)}, s32[1,64]{1,0:T(1,128)}, u32[]{:S(2)}) copy-start(s32[1,64]{1,0:T(1,128)} %param.14) | copy-start | bytes 772
  135.7 9.5 %copy-start.22 = (s32[1,4]{1,0:T(1,128)S(1)}, s32[1,4]{1,0:T(1,128)}, u32[]{:S(2)}) copy-start(s32[1,4]{1,0:T(1,128)} %param.17) | copy-start | bytes 52
  135.7 10.1 %copy-start.20 = (s32[1,64]{1,0:T(1,128)S(1)}, s32[1,64]{1,0:T(1,128)}, u32[]{:S(2)}) copy-start(s32[1,64]{1,0:T(1,128)} %param.16) | copy-start | bytes 772
  135.7 10.6 %copy-start.17 = (f32[1,4,256]{2,1,0:T(4,128)S(1)}, f32[1,4,256]{2,1,0:T(4,128)}, u32[]{:S(2)}) copy-start(f32[1,4,256]{2,1,0:T(4,128)} %param.18) | copy-start | bytes 12292
  135.7 11.9 %copy-start.12 = (f32[8,8,8,8]{3,2,1,0:T(8,128)S(1)}, f32[8,8,8,8]{3,2,1,0:T(8,128)}, u32[]{:S(2)}) copy-start(f32[8,8,8,8]{3,2,1,0:T(8,128)} %div.90) | copy-start | bytes 49156
  135.7 11.9 %copy-start.13 = (f32[8,8,8,8]{3,2,1,0:T(8,128)S(1)}, f32[8,8,8,8]{3,2,1,0:T(8,128)}, u32[]{:S(2)}) copy-start(f32[8,8,8,8]{3,2,1,0:T(8,128)} %rsqrt.68) | copy-start | bytes 49156
  146.3 6.2 copy-start.16
  147.6 4.8 copy-start.9
  152.5 241.8 %copy-start.2 = (s32[1,64]{1,0:T(1,128)S(1)}, s32[1,64]{1,0:T(1,128)}, u32[]{:S(2)}) copy-start(s32[1,64]{1,0:T(1,128)} %param.15) | copy-start | bytes 772
  152.5 5.9 copy-start.18
  171.3 5.9 copy-start.4
  172.7 7.8 %copy-start.19 = (f32[8,8,1]{1,2,0:T(1,128)S(1)}, f32[8,8,1]{1,2,0:T(1,128)}, u32[]{:S(2)}) copy-start(f32[8,8,1]{1,2,0:T(1,128)} %copy-done.18) | copy-start | bytes 772 | tf_op jit(solution)/shard_map/while
  180.5 5.9 copy-start.18
  199.4 8.1 %copy-start.4 = (f32[768,384]{1,0:T(8,128)S(1)}, f32[768,384]{1,0:T(8,128)}, u32[]{:S(2)}) copy-start(f32[768,384]{1,0:T(8,128)} %get-tuple-element.842) | copy-start | bytes 3538948 | tf_op jit(solution)/shard_map/while
  200.8 10.0 %copy-start.19 = (f32[8,8,1]{1,2,0:T(1,128)S(1)}, f32[8,8,1]{1,2,0:T(1,128)}, u32[]{:S(2)}) copy-start(f32[8,8,1]{1,2,0:T(1,128)} %copy-done.18) | copy-start | bytes 772 | tf_op jit(solution)/shard_map/while
  209.7 1.0 copy-start.5
  210.7 5.9 copy-start.18
  229.6 8.1 %copy-start.4 = (f32[768,384]{1,0:T(8,128)S(1)}, f32[768,384]{1,0:T(8,128)}, u32[]{:S(2)}) copy-start(f32[768,384]{1,0:T(8,128)} %get-tuple-element.842) | copy-start | bytes 3538948 | tf_op jit(solution)/shard_map/while
  231.0 10.0 %copy-start.19 = (f32[8,8,1]{1,2,0:T(1,128)S(1)}, f32[8,8,1]{1,2,0:T(1,128)}, u32[]{:S(2)}) copy-start(f32[8,8,1]{1,2,0:T(1,128)} %copy-done.18) | copy-start | bytes 772 | tf_op jit(solution)/shard_map/while
  240.9 5.9 copy-start.18
  259.8 8.1 %copy-start.4 = (f32[768,384]{1,0:T(8,128)S(1)}, f32[768,384]{1,0:T(8,128)}, u32[]{:S(2)}) copy-start(f32[768,384]{1,0:T(8,128)} %get-tuple-element.842) | copy-start | bytes 3538948 | tf_op jit(solution)/shard_map/while
  261.1 10.0 %copy-start.19 = (f32[8,8,1]{1,2,0:T(1,128)S(1)}, f32[8,8,1]{1,2,0:T(1,128)}, u32[]{:S(2)}) copy-start(f32[8,8,1]{1,2,0:T(1,128)} %copy-done.18) | copy-start | bytes 772 | tf_op jit(solution)/shard_map/while
  271.1 5.9 copy-start.18
  289.9 8.1 %copy-start.4 = (f32[768,384]{1,0:T(8,128)S(1)}, f32[768,384]{1,0:T(8,128)}, u32[]{:S(2)}) copy-start(f32[768,384]{1,0:T(8,128)} %get-tuple-element.842) | copy-start | bytes 3538948 | tf_op jit(solution)/shard_map/while
  291.3 10.0 %copy-start.19 = (f32[8,8,1]{1,2,0:T(1,128)S(1)}, f32[8,8,1]{1,2,0:T(1,128)}, u32[]{:S(2)}) copy-start(f32[8,8,1]{1,2,0:T(1,128)} %copy-done.18) | copy-start | bytes 772 | tf_op jit(solution)/shard_map/while
  300.2 1.0 copy-start.5
  301.3 5.9 copy-start.18
  320.1 8.1 %copy-start.4 = (f32[768,384]{1,0:T(8,128)S(1)}, f32[768,384]{1,0:T(8,128)}, u32[]{:S(2)}) copy-start(f32[768,384]{1,0:T(8,128)} %get-tuple-element.842) | copy-start | bytes 3538948 | tf_op jit(solution)/shard_map/while
  321.5 10.0 %copy-start.19 = (f32[8,8,1]{1,2,0:T(1,128)S(1)}, f32[8,8,1]{1,2,0:T(1,128)}, u32[]{:S(2)}) copy-start(f32[8,8,1]{1,2,0:T(1,128)} %copy-done.18) | copy-start | bytes 772 | tf_op jit(solution)/shard_map/while
  331.4 5.9 copy-start.18
  350.3 8.1 %copy-start.4 = (f32[768,384]{1,0:T(8,128)S(1)}, f32[768,384]{1,0:T(8,128)}, u32[]{:S(2)}) copy-start(f32[768,384]{1,0:T(8,128)} %get-tuple-element.842) | copy-start | bytes 3538948 | tf_op jit(solution)/shard_map/while
  351.6 10.0 %copy-start.19 = (f32[8,8,1]{1,2,0:T(1,128)S(1)}, f32[8,8,1]{1,2,0:T(1,128)}, u32[]{:S(2)}) copy-start(f32[8,8,1]{1,2,0:T(1,128)} %copy-done.18) | copy-start | bytes 772 | tf_op jit(solution)/shard_map/while
  360.6 1.0 copy-start.5
  361.6 5.9 copy-start.18
  380.4 8.1 %copy-start.4 = (f32[768,384]{1,0:T(8,128)S(1)}, f32[768,384]{1,0:T(8,128)}, u32[]{:S(2)}) copy-start(f32[768,384]{1,0:T(8,128)} %get-tuple-element.842) | copy-start | bytes 3538948 | tf_op jit(solution)/shard_map/while
  381.8 10.0 %copy-start.19 = (f32[8,8,1]{1,2,0:T(1,128)S(1)}, f32[8,8,1]{1,2,0:T(1,128)}, u32[]{:S(2)}) copy-start(f32[8,8,1]{1,2,0:T(1,128)} %copy-done.18) | copy-start | bytes 772 | tf_op jit(solution)/shard_map/while
  391.8 293.3 %copy-start.1 = (f32[384,256]{1,0:T(8,128)S(1)}, f32[384,256]{1,0:T(8,128)}, u32[]{:S(2)}) copy-start(f32[384,256]{1,0:T(8,128)} %param.23) | copy-start | bytes 1179652
  395.9 119.0 %all-to-all-start.1 = ((s32[32,2,1]{1,2,0:T(1,128)}), s32[32,2,1]{1,2,0:T(1,128)S(1)}, u32[]{:S(2)}, u32[]{:S(2)}) async-start(s32[32,2,1]{1,2,0:T(1,128)} %bitcast.63), calls=%async_computation.1 | async-start | bytes 32768 | tf_op jit(solution)/shard_map/all_to_all | solution.py:206
  514.9 15.3 %all-to-all-start = ((f32[32,2,384]{2,1,0:T(2,128)}), f32[32,2,384]{2,1,0:T(2,128)S(1)}, u32[]{:S(2)}, u32[]{:S(2)}) async-start(f32[32,2,384]{2,1,0:T(2,128)} %broadcast_select_fusion), calls=%async_computation | async-start | bytes 196608 | tf_op jit(solution)/shard_map/all_to_all | solution.py:219
  (6 other events, 5.7 us)
Sparse Core Ops, SparseCore 0:
  391.9 286.9 all-reduce.4
where the time goes:
time: 698 us; the launch traced here: 692 us
  other arithmetic  189 us (27%)
  waiting for transfers between devices  155 us (22%)
  local copies, waits for them, and re-layouts  112 us (16%)
  blocking collectives  106 us (15%)
  matrix products  96.2 us (14%)
  starting transfers between devices  16.8 us (2%)
  between operations  14.3 us (2%)
    psum x1, waiting for transfers between devices, local(): lax.psum((found[0], found[1], found[2], found[3]), ('bulk', 'slide'))  147 us
    psum x1, blocking collectives, local(): lax.psum((found[0], found[1], found[2], found[3]), ('bulk', 'slide'))  106 us
    reduce_sum x1, other arithmetic, norm_rows(): centered = values - jnp.mean(values, axis=-1, keepdims=True)  81.2 us
    dynamic_slice x40, local copies, waits for them, and re-layouts, blocked_gradients(): lax.scan(advance, start, (split_rows(images), jax.tree.map(split_rows, sa...  36.5 us
    reduce_sum x24, other arithmetic, gradients(): tap_list.append(jnp.sum(window * back_spatial, axis=(0, 1, 2)))  36.1 us
    dot_general x8, matrix products, gradients(): jnp.dot(pooled_patch.T, back_reduced, precision=lax.Precision.HIGHEST)  18.1 us
    reduce_sum x16, other arithmetic, norm_back(): jnp.mean(incoming * normed, axis=-1, keepdims=True)  17.8 us
    dot_general x8, matrix products, gradients(): jnp.dot(active.T, summed_low, preferred_element_type=jnp.float32)  17.1 us
  transfers between devices with their start and end apart: 3, of which 2 were waited for; matrix products, arithmetic and copies ran while one was open for 1% of the time, Pallas kernels for 0%

commit v1 on v0

v1 whole, which is shorter than its diff:
```python
import functools
import jax
import jax.numpy as jnp
from jax import lax
from jax.experimental import pallas as pl
from jax.experimental.pallas import tpu as pltpu
from jax.sharding import PartitionSpec as P

F32 = jnp.float32
BF = jnp.bfloat16
TILES = 64
CHANS = 192
HIDDEN = 768
WIDTH = 384
GROUPS = 6
PLANE = 8 * TILES
norm_eps = 1e-06


def dot(a, b):
    return jnp.dot(a, b, preferred_element_type=F32)


def dot_nt(a, b):
    return lax.dot_general(a, b, (((1,), (1,)), ((), ())), preferred_element_type=F32)


def dot_tn(a, b):
    return lax.dot_general(a, b, (((0,), (0,)), ((), ())), preferred_element_type=F32)


def parts_of(values):
    high = values.astype(BF)
    rest = values - high.astype(F32)
    middle = rest.astype(BF)
    low = (rest - middle.astype(F32)).astype(BF)
    return high, middle, low


def lane_mean(values):
    return jnp.sum(values, axis=-1, keepdims=True) * (1.0 / values.shape[-1])


def norm_rows(values):
    centered = values - lane_mean(values)
    factor = lax.rsqrt(lane_mean(centered * centered) + norm_eps)
    return centered * factor, factor


def gelu_pair(h):
    size = jnp.abs(h)
    bell = jnp.exp(h * h * -0.5)
    t = 1.0 / (1.0 + (0.3275911 * 0.7071067811865476) * size)
    poly = t * (
        0.5 * 0.254829592
        + t
        * (
            0.5 * -0.284496736
            + t * (0.5 * 1.421413741 + t * (0.5 * -1.453152027 + t * (0.5 * 1.061405429)))
        )
    )
    tail = poly * bell
    phi = jnp.where(h >= 0, 1.0 - tail, tail)
    return h * phi, phi + h * bell * 0.3989422804014327


def gelu_pair_erf(h):
    phi = 0.5 * (1.0 + lax.erf(h * 0.7071067811865476))
    return h * phi, phi + h * jnp.exp(h * h * -0.5) * 0.3989422804014327


GELU = gelu_pair


def blocks_of_lanes(rows):
    return lax.broadcasted_iota(jnp.int32, (rows, 128), 1) // 32


def to_groups(source, target, row0):
    block = blocks_of_lanes(TILES)

    def step(i, carry):
        for t in range(2):
            tiles = []
            for jm in range(4):
                rows = pl.ds((4 * t + jm) * PLANE + i * TILES, TILES)
                tiles.append((source[rows, 0:128], source[rows, 128:256]))
            for g in range(GROUPS):
                total = None
                for jm in range(4):
                    shift = 32 * ((jm - g % 4) % 4)
                    piece = tiles[jm][g // 4]
                    if shift:
                        piece = pltpu.roll(piece, shift, 1)
                    total = piece if total is None else jnp.where(block == jm, piece, total)
                target[g, pl.ds(row0 + i * TILES, TILES), t * 128 : (t + 1) * 128] = total.astype(BF)
        return carry

    lax.fori_loop(0, 8, step, 0)


def compute_kernel(
    x_ref, taps_ref, w1_ref, w2t_ref, wr_ref, head_ref, dest_ref, slot_ref, slide_ref, count_ref, targets_ref,
    pred_ref, send_ref, pack_ref,
    g1_ref, g2_ref, gr_ref, low_ref, high_ref, xs_ref, xg_ref, xt_ref, wd_ref, tg_ref, y_ref, n_ref, nb_ref,
    gb_ref, sl_ref, m_ref, pm_ref, w1t_ref, w2_ref, bp_ref, fold_ref,
):
    f1_ref, f2_ref, gy_ref = low_ref, high_ref, xs_ref

    def widen(k, carry):
        rows = pl.ds(k * 512, 512)
        values = x_ref[rows, :].astype(F32)
        low_ref[rows, :] = values[:, 0:128]
        high_ref[rows, 0:64] = values[:, 128:192]
        return carry

    lax.fori_loop(0, 8, widen, 0)

    def regroup(i, carry):
        for j in range(8):
            rows = pl.ds(j * PLANE + i * TILES, TILES)
            xs_ref[rows, 0:128] = low_ref[pl.ds(i * 8 + j, TILES, stride=64), :]
            xs_ref[rows, 128:256] = high_ref[pl.ds(i * 8 + j, TILES, stride=64), :]
        return carry

    lax.fori_loop(0, 8, regroup, 0)

    xg_ref[:, 0 : 3 * TILES, :] = jnp.zeros((GROUPS, 3 * TILES, 256), BF)
    xg_ref[:, 11 * TILES : 14 * TILES, :] = jnp.zeros((GROUPS, 3 * TILES, 256), BF)
    to_groups(xs_ref, xg_ref, 3 * TILES)

    block56 = blocks_of_lanes(56)
    taps_low = taps_ref[:, 0:128]
    taps_high = taps_ref[:, 128:256]
    for g in range(GROUPS):
        source = taps_low if g < 4 else taps_high
        total = None
        for jm in range(4):
            shift = 32 * ((jm - g % 4) % 4)
            piece = pltpu.roll(source, shift, 1) if shift else source
            total = piece if total is None else jnp.where(block56 == jm, piece, total)
        for a in range(7):
            tg_ref[g, a, 0:4, :] = jnp.zeros((4, 128), F32)
            tg_ref[g, a, 4:11, :] = total[a * 7 : a * 7 + 7, :]
            tg_ref[g, a, 11:16, :] = jnp.zeros((5, 128), F32)
    same = lax.broadcasted_iota(jnp.int32, (32, 128), 0) == lax.broadcasted_iota(jnp.int32, (32, 128), 1) % 32
    block32 = blocks_of_lanes(32)

    def bands(g):
        for a in range(7):
            for d in range(-4, 8):
                total = None
                for jm in range(4):
                    b = d - jm + 3
                    if b < 0 or b > 6:
                        continue
                    row = jnp.broadcast_to(tg_ref[g, a, 4 + b : 5 + b, :], (32, 128))
                    keep = same & (block32 == jm)
                    total = jnp.where(keep, row, 0.0) if total is None else jnp.where(keep, row, total)
                if total is None:
                    total = jnp.zeros((32, 128), F32)
                pieces = parts_of(total)[:SPLIT]
                for p in range(SPLIT):
                    if d >= 0:
                        wd_ref[a, p, d * 32 : d * 32 + 32, 0:128] = pieces[p]
                    if d + 4 < 8:
                        wd_ref[a, p, (d + 4) * 32 : (d + 4) * 32 + 32, 128:256] = pieces[p]

    def convolve(g, carry):
        bands(g)
        total = None
        for a in range(7):
            lhs = xg_ref[g, a * TILES : a * TILES + PLANE, :]
            for p in range(SPLIT):
                found = dot(lhs, wd_ref[a, p])
                total = found if total is None else total + found
        y_ref[g] = total
        xt_ref[g, 0, :, 128:768] = jnp.transpose(xg_ref[g, 128:768, :], (1, 0))
        xt_ref[g, 1, :, 128:640] = jnp.transpose(xg_ref[g, 192:704, :], (1, 0))
        xt_ref[g, 0, :, 0:128] = jnp.zeros((256, 128), BF)
        xt_ref[g, 0, :, 768:896] = jnp.zeros((256, 128), BF)
        xt_ref[g, 1, :, 0:128] = jnp.zeros((256, 128), BF)
        xt_ref[g, 1, :, 640:896] = jnp.zeros((256, 256), BF)
        return carry

    lax.fori_loop(0, GROUPS, convolve, 0)

    block64 = blocks_of_lanes(TILES)

    def first_norm(i, carry):
        rows = pl.ds(i * TILES, TILES)
        for t in range(2):
            tiles = [y_ref[g, rows, t * 128 : (t + 1) * 128] for g in range(GROUPS)]
            for jm in range(4):
                halves = []
                for picks in ((0, 1, 2, 3), (4, 5)):
                    total = None
                    for g in picks:
                        shift = 32 * ((g % 4 - jm) % 4)
                        piece = pltpu.roll(tiles[g], shift, 1) if shift else tiles[g]
                        total = piece if total is None else jnp.where(block64 == g % 4, piece, total)
                    halves.append(total)
                halves[1] = jnp.where(block64 < 2, halves[1], 0.0)
                mean = jnp.sum(halves[0] + halves[1], axis=-1, keepdims=True) * (1.0 / CHANS)
                c0 = halves[0] - mean
                c1 = jnp.where(block64 < 2, halves[1] - mean, 0.0)
                factor = lax.rsqrt(jnp.sum(c0 * c0 + c1 * c1, axis=-1, keepdims=True) * (1.0 / CHANS) + norm_eps)
                where = pl.ds((4 * t + jm) * PLANE + i * TILES, TILES)
                n0 = c0 * factor
                n1 = c1 * factor
                n_ref[where, 0:128] = n0
                n_ref[where, 128:256] = n1
                nb_ref[where, 0:128] = n0.astype(BF)
                nb_ref[where, 128:256] = n1.astype(BF)
                f1_ref[where, :] = jnp.broadcast_to(factor, (TILES, 128))
        return carry

    lax.fori_loop(0, 8, first_norm, 0)

    pm_ref[...] = jnp.zeros_like(pm_ref)
    w1t_ref[...] = jnp.transpose(w1_ref[...], (1, 0))
    w2_ref[...] = jnp.transpose(w2t_ref[...], (1, 0))

    def block_step(k, carry):
        rows = pl.ds(k * CH, CH)
        low = nb_ref[rows, 0:CHANS]
        branch = None
        for part in range(HIDDEN // HP):
            cols = slice(part * HP, part * HP + HP)
            hidden = dot(low, w1_ref[:, cols])
            active, slope = GELU(hidden)
            active = active.astype(BF)
            gb_ref[rows, cols] = active
            sl_ref[rows, cols] = slope.astype(BF)
            found = dot(active, w2_ref[cols, :])
            branch = found if branch is None else branch + found
        summed = xs_ref[rows, 0:CHANS] + branch
        normed, factor = norm_rows(summed)
        m_ref[rows, 0:CHANS] = normed
        f2_ref[rows, :] = jnp.broadcast_to(factor, (CH, 128))
        rounded = normed.astype(BF).astype(F32)
        lateral = lax.rem(k // (PLANE // CH), 2)
        for u in range(2):
            total = None
            for i in range(u, CH // TILES, 2):
                piece = rounded[i * TILES : (i + 1) * TILES, :]
                total = piece if total is None else total + piece
            pm_ref[u, lateral] += total
        return carry

    lax.fori_loop(0, 8 * PLANE // CH, block_step, 0)

    pooled = [pm_ref[u, v] * (1.0 / 16.0) for u in range(2) for v in range(2)]
    split = [parts_of(piece) for piece in pooled]
    reduced = None
    for q in range(4):
        stacked = jnp.concatenate(split[q], axis=0)
        found = dot(stacked, wr_ref[q * CHANS : (q + 1) * CHANS, :])
        found = found[0:TILES] + found[TILES : 2 * TILES] + found[2 * TILES :]
        reduced = found if reduced is None else reduced + found
    embedded, third = norm_rows(reduced)
    slide_row = slide_ref[...]
    member = (slide_row == lax.broadcasted_iota(jnp.int32, (8, TILES), 0)).astype(F32)
    eye = lax.broadcasted_iota(jnp.int32, (TILES, TILES), 0) == lax.broadcasted_iota(jnp.int32, (TILES, TILES), 1)
    eye8 = lax.broadcasted_iota(jnp.int32, (8, 8), 0) == lax.broadcasted_iota(jnp.int32, (8, 8), 1)
    counts = jnp.sum(jnp.where(eye8, jnp.broadcast_to(count_ref[...].astype(F32), (8, 8)), 0.0), axis=1, keepdims=True)
    exact = functools.partial(jnp.dot, precision=lax.Precision.HIGHEST, preferred_element_type=F32)
    pooled_slides = exact(member, embedded) / counts
    predicted = exact(pooled_slides, head_ref[...])
    pred_ref[...] = predicted[0:4]
    missed = predicted[0:4] - targets_ref[...]
    missed = jnp.concatenate([missed, jnp.zeros((4, missed.shape[1]), F32)], axis=0)
    back_pooled = (
        lax.dot_general(
            missed, head_ref[...], (((1,), (1,)), ((), ())), precision=lax.Precision.HIGHEST, preferred_element_type=F32
        )
        / counts
    )
    cotangent = lax.dot_general(
        member, back_pooled, (((0,), (0,)), ((), ())), precision=lax.Precision.HIGHEST, preferred_element_type=F32
    )
    back = third * (cotangent - lane_mean(cotangent) - embedded * lane_mean(cotangent * embedded))
    back_parts = parts_of(back)
    stacked_back = jnp.concatenate(back_parts, axis=0)
    for q in range(4):
        piece = dot_nt(stacked_back, wr_ref[q * CHANS : (q + 1) * CHANS, :])
        piece = (piece[0:TILES] + piece[TILES : 2 * TILES] + piece[2 * TILES :]) * (1.0 / 16.0)
        bp_ref[q // 2, q % 2] = piece
        rows_q = jnp.concatenate([split[q][0], split[q][1], split[q][0]], axis=0)
        cols_q = jnp.concatenate([back_parts[0], back_parts[0], back_parts[1]], axis=0)
        gr_ref[q * CHANS : (q + 1) * CHANS, :] = dot_tn(rows_q, cols_q)

    dest_row = dest_ref[...]
    dest_col = jnp.sum(jnp.where(eye, jnp.broadcast_to(dest_row, (TILES, TILES)).astype(F32), 0.0), axis=1, keepdims=True)
    first_index = lax.broadcasted_iota(jnp.int32, (TILES, TILES), 0)
    second_index = lax.broadcasted_iota(jnp.int32, (TILES, TILES), 1)
    dest_f = dest_row.astype(F32)
    earlier = (dest_col == dest_f) & (first_index < second_index)
    rank = jnp.sum(earlier.astype(F32), axis=0, keepdims=True)
    slot_f = slot_ref[...].astype(F32) + 1.0
    slot_col = jnp.sum(jnp.where(eye, jnp.broadcast_to(slot_f, (TILES, TILES)), 0.0), axis=1, keepdims=True)
    emb_parts = parts_of(embedded)
    peer = lax.broadcasted_iota(jnp.int32, (32, TILES), 0).astype(F32)
    for r in range(2):
        choose = ((peer == dest_f) & (rank == float(r))).astype(BF)
        picked = dot(choose, emb_parts[0]) + dot(choose, emb_parts[1]) + dot(choose, emb_parts[2])
        for q in range(3):
            send_ref[pl.ds(r * 4 + q, 32, stride=8), :] = picked[:, q * 128 : (q + 1) * 128]
        send_ref[pl.ds(r * 4 + 3, 32, stride=8), :] = dot(choose, jnp.broadcast_to(slot_col, (TILES, 128)).astype(BF))

    g1_ref[...] = jnp.zeros_like(g1_ref)
    g2_ref[...] = jnp.zeros_like(g2_ref)

    def back_step(k, carry):
        rows = pl.ds(k * CH, CH)
        lateral = lax.rem(k // (PLANE // CH), 2)
        patch = [bp_ref[u, lateral] for u in range(2)]
        incoming = jnp.concatenate([patch[i % 2] for i in range(CH // TILES)], axis=0)
        normed = m_ref[rows, 0:CHANS]
        factor = f2_ref[rows, 0:1]
        back_sum = factor * (incoming - lane_mean(incoming) - normed * lane_mean(incoming * normed))
        low = back_sum.astype(BF)
        active = gb_ref[rows, :]
        g2_ref[...] += dot_tn(low, active)
        nb = nb_ref[rows, 0:CHANS]
        normal = None
        for part in range(HIDDEN // HP):
            cols = slice(part * HP, part * HP + HP)
            back_hidden = (dot(low, w2t_ref[:, cols]) * sl_ref[rows, cols].astype(F32)).astype(BF)
            g1_ref[:, cols] += dot_tn(nb, back_hidden)
            found = dot(back_hidden, w1t_ref[cols, :])
            normal = found if normal is None else normal + found
        n = n_ref[rows, 0:CHANS]
        f1 = f1_ref[rows, 0:1]
        gy_ref[rows, 0:CHANS] = f1 * (normal - lane_mean(normal) - n * lane_mean(normal * n))
        return carry

    lax.fori_loop(0, 8 * PLANE // CH, back_step, 0)

    to_groups(gy_ref, xg_ref, 0)
    block8 = blocks_of_lanes(8)
    same8 = [
        (lax.broadcasted_iota(jnp.int32, (8, 128), 0) + 8 * v) == lax.broadcasted_iota(jnp.int32, (8, 128), 1) % 32
        for v in range(4)
    ]

    def tap_step(g, carry):
        right = xg_ref[g, 0:PLANE, :]
        for a in range(7):
            lane0 = (a * TILES) // 128 * 128
            left = xt_ref[g, a % 2, :, lane0 : lane0 + PLANE]
            found = dot(left, right)
            sums = {}
            for j in range(8):
                for t in range(2):
                    total = None
                    for v in range(4):
                        piece = found[j * 32 + v * 8 : j * 32 + v * 8 + 8, t * 128 : (t + 1) * 128]
                        piece = jnp.where(same8[v], piece, 0.0)
                        total = piece if total is None else total + piece
                    sums[j, t] = total
            for b in range(7):
                total = None
                for t in range(2):
                    inner = jnp.zeros((8, 128), F32)
                    for jm in range(4):
                        j = 4 * t + jm + b - 3
                        if 0 <= j < 8:
                            inner = jnp.where(block8 == jm, sums[j, t], inner)
                    total = inner if total is None else total + inner
                total = total + pltpu.roll(total, 64, 1)
                total = total + pltpu.roll(total, 32, 1)
                fold_ref[g, a * 7 + b : a * 7 + b + 1, :] = jnp.sum(total, axis=0, keepdims=True)
        return carry

    lax.fori_loop(0, GROUPS, tap_step, 0)
    block49 = blocks_of_lanes(56)
    for half, picks in enumerate(((0, 1, 2, 3), (4, 5))):
        total = jnp.zeros((56, 128), F32)
        for g in picks:
            total = jnp.where(block49 == g % 4, fold_ref[g], total)
        for band in range(7):
            pack_ref[band * 2 + half, 72:80, :] = total[band * 8 : band * 8 + 8, :]
    pack_ref[14:64, 72:80, :] = jnp.zeros((50, 8, 128), F32)
    for k in range(32):
        for l in range(3):
            pack_ref[k, l * 24 : l * 24 + 24, :] = gr_ref[k * 24 : k * 24 + 24, l * 128 : l * 128 + 128]
    for k in range(16):
        for l in range(3):
            lane = (k % 2) * 384 + l * 128
            row = k // 2 * 24
            pack_ref[32 + k, l * 24 : l * 24 + 24, :] = g1_ref[row : row + 24, lane : lane + 128]
            pack_ref[48 + k, l * 24 : l * 24 + 24, :] = g2_ref[row : row + 24, lane : lane + 128]


SPLIT = 2
CH = 512
HP = 256


def compute(x, taps, w1, w2t, wr, head, dest, slot, slide, count, targets):
    shapes = (
        jax.ShapeDtypeStruct((4, 256), F32),
        jax.ShapeDtypeStruct((256, 128), F32),
        jax.ShapeDtypeStruct((64, 80, 128), F32),
    )
    rows = 8 * PLANE
    scratch = [
        pltpu.VMEM((CHANS, HIDDEN), F32),
        pltpu.VMEM((CHANS, HIDDEN), F32),
        pltpu.VMEM((4 * CHANS, WIDTH), F32),
        pltpu.VMEM((rows, 128), F32),
        pltpu.VMEM((rows, 128), F32),
        pltpu.VMEM((rows, 256), F32),
        pltpu.VMEM((GROUPS, 14 * TILES, 256), BF),
        pltpu.VMEM((GROUPS, 2, 256, 896), BF),
        pltpu.VMEM((7, SPLIT, 256, 256), BF),
        pltpu.VMEM((GROUPS, 7, 16, 128), F32),
        pltpu.VMEM((GROUPS, PLANE, 256), F32),
        pltpu.VMEM((rows, 256), F32),
        pltpu.VMEM((rows, 256), BF),
        pltpu.VMEM((rows, HIDDEN), BF),
        pltpu.VMEM((rows, HIDDEN), BF),
        pltpu.VMEM((rows, 256), F32),
        pltpu.VMEM((2, 2, TILES, CHANS), F32),
        pltpu.VMEM((HIDDEN, CHANS), BF),
        pltpu.VMEM((HIDDEN, CHANS), BF),
        pltpu.VMEM((2, 2, TILES, CHANS), F32),
        pltpu.VMEM((GROUPS, 56, 128), F32),
    ]
    return pl.pallas_call(
        compute_kernel,
        out_shape=shapes,
        in_specs=[pl.BlockSpec(memory_space=pltpu.VMEM)] * 11,
        out_specs=tuple(pl.BlockSpec(memory_space=pltpu.VMEM) for _ in shapes),
        scratch_shapes=scratch,
        compiler_params=pltpu.CompilerParams(vmem_limit_bytes=62 * 1024 * 1024),
        name="encode_and_gradients",
    )(x, taps, w1, w2t, wr, head, dest, slot, slide, count, targets)


def sum_kernel(pack_ref, send_ref, all_ref, got_ref, core_out, core_in, own_ref, x_out, x_in, y_out, y_in, z_out, z_in, send_sems, recv_sems):
    bulk = lax.axis_index("bulk")
    slide = lax.axis_index("slide")
    x, y = bulk // 8, bulk % 8
    z, core = slide // 2, slide % 2

    def place(bx, by, bz, bc):
        return (bx * 8 + by, bz * 2 + bc)

    mate = place(x, y, z, 1 - core)
    x_peers = [((x + o) % 4) for o in range(1, 4)]
    y_peers = [((y + o) % 8) for o in range(1, 8)]
    z_peers = [((z + o) % 8) for o in range(1, 8)]
    b_peers = [((bulk + o) % 32) for o in range(1, 32)]
    barrier = pltpu.get_barrier_semaphore()
    everyone = [mate] + [(b, slide) for b in b_peers] + [place(x, y, p, core) for p in z_peers]
    for device in everyone:
        pl.semaphore_signal(barrier, inc=1, device_id=device, device_id_type=pl.DeviceIdType.MESH)
    counter = [0]

    def copy(source, target, device):
        k = counter[0]
        counter[0] += 1
        made = pltpu.make_async_remote_copy(
            src_ref=source, dst_ref=target, send_sem=send_sems.at[k], recv_sem=recv_sems.at[k],
            device_id=device, device_id_type=pl.DeviceIdType.MESH,
        )
        made.start()
        return made

    def finish(copies):
        for made in copies:
            made.wait_recv()

    def pack(k, carry):
        core_out[k] = pack_ref[(1 - core) * 32 + k].astype(BF)
        return carry

    lax.fori_loop(0, 32, pack, 0, unroll=8)
    pl.semaphore_wait(barrier, len(everyone))
    started = [copy(core_out, core_in, mate)]
    tiles = [copy(send_ref.at[p], got_ref.at[bulk], (p, slide)) for p in b_peers]
    got_ref[bulk] = send_ref[bulk]
    finish(started)

    def add_core(k, carry):
        total = pack_ref[core * 32 + k] + core_in[k].astype(F32)
        own_ref[k] = total
        x_out[k // 8, k % 8] = total.astype(BF)
        return carry

    lax.fori_loop(0, 32, add_core, 0, unroll=8)
    step = [copy(x_out.at[p], x_in.at[o], place(p, y, z, core)) for o, p in enumerate(x_peers)]
    started += step
    finish(step)

    def add_x(k, carry):
        total = own_ref[x * 8 + k]
        for o in range(3):
            total = total + x_in[o, k].astype(F32)
        y_out[k] = total.astype(YT)
        return carry

    lax.fori_loop(0, 8, add_x, 0, unroll=4)
    step = [copy(y_out.at[p], y_in.at[o], place(x, p, z, core)) for o, p in enumerate(y_peers)]
    started += step
    finish(step)
    total = y_out[y].astype(F32)
    for o in range(7):
        total = total + y_in[o].astype(F32)
    z_out[...] = total.astype(ZT)
    step = [copy(z_out, z_in.at[z], place(x, y, p, core)) for p in z_peers]
    started += step
    z_in[z] = z_out[...]
    finish(step)
    total = z_in[0].astype(F32)
    for o in range(1, 8):
        total = total + z_in[o].astype(F32)
    mine = core * 32 + x * 8 + y
    all_ref[mine] = total.astype(BF)
    step = [copy(all_ref.at[mine], all_ref.at[mine], place(x, p, z, core)) for p in y_peers]
    started += step
    finish(step)
    row = all_ref.at[pl.ds(core * 32 + x * 8, 8)]
    step = [copy(row, row, place(p, y, z, core)) for p in x_peers]
    started += step
    finish(step)
    half = all_ref.at[pl.ds(core * 32, 32)]
    step = [copy(half, half, mate)]
    started += step
    finish(step)
    finish(tiles)
    for made in started + tiles:
        made.wait_send()


YT = F32
ZT = F32


def sum_everywhere(pack, send):
    vmem = pl.BlockSpec(memory_space=pltpu.VMEM)
    return pl.pallas_call(
        sum_kernel,
        out_shape=(jax.ShapeDtypeStruct((64, 80, 128), BF), jax.ShapeDtypeStruct((32, 8, 128), F32)),
        in_specs=[vmem, vmem],
        out_specs=(vmem, vmem),
        scratch_shapes=[
            pltpu.VMEM((32, 80, 128), BF),
            pltpu.VMEM((32, 80, 128), BF),
            pltpu.VMEM((32, 80, 128), F32),
            pltpu.VMEM((4, 8, 80, 128), BF),
            pltpu.VMEM((3, 8, 80, 128), BF),
            pltpu.VMEM((8, 80, 128), YT),
            pltpu.VMEM((7, 80, 128), YT),
            pltpu.VMEM((80, 128), ZT),
            pltpu.VMEM((8, 80, 128), ZT),
            pltpu.SemaphoreType.DMA((60,)),
            pltpu.SemaphoreType.DMA((60,)),
        ],
        compiler_params=pltpu.CompilerParams(
            collective_id=0, has_side_effects=True, vmem_limit_bytes=40 * 1024 * 1024
        ),
        name="sum_gradients",
    )(pack, send.reshape(32, 8, 128))


def unpack_kernel(all_ref, got_ref, cache_ref, gt_ref, g1_ref, g2_ref, gr_ref):
    for k in range(32):
        values = all_ref[k, 0:72, :].astype(F32)
        for l in range(3):
            gr_ref[k * 24 : k * 24 + 24, l * 128 : l * 128 + 128] = values[l * 24 : l * 24 + 24]
    for k in range(16):
        first = all_ref[32 + k, 0:72, :].astype(F32)
        second = all_ref[48 + k, 0:72, :].astype(F32)
        for l in range(3):
            lane = (k % 2) * 384 + l * 128
            row = k // 2 * 24
            g1_ref[row : row + 24, lane : lane + 128] = first[l * 24 : l * 24 + 24]
            g2_ref[row : row + 24, lane : lane + 128] = second[l * 24 : l * 24 + 24]
    for band in range(7):
        left = all_ref[band * 2].astype(F32)[72:80]
        right = all_ref[band * 2 + 1].astype(F32)[72:80]
        count = 8 if band < 6 else 1
        gt_ref[band * 8 : band * 8 + count, 0:128] = left[0:count]
        gt_ref[band * 8 : band * 8 + count, 128:192] = right[0:count, 0:64]
    cache = [jnp.zeros((24, 128), F32) for _ in range(3)]
    for r in range(2):
        slots = jnp.transpose(got_ref[pl.ds(r * 4 + 3, 32, stride=8), :], (1, 0))[0:24]
        wanted = (lax.broadcasted_iota(jnp.int32, (24, 32), 0) + 1).astype(F32)
        choose = (slots == wanted).astype(BF)
        for q in range(3):
            for piece in parts_of(got_ref[pl.ds(r * 4 + q, 32, stride=8), :]):
                cache[q] = cache[q] + dot(choose, piece)
    for q in range(3):
        cache_ref[:, q * 128 : (q + 1) * 128] = cache[q]


def unpack(everything, got):
    vmem = pl.BlockSpec(memory_space=pltpu.VMEM)
    return pl.pallas_call(
        unpack_kernel,
        out_shape=(
            jax.ShapeDtypeStruct((24, WIDTH), F32),
            jax.ShapeDtypeStruct((49, CHANS), F32),
            jax.ShapeDtypeStruct((CHANS, HIDDEN), F32),
            jax.ShapeDtypeStruct((CHANS, HIDDEN), F32),
            jax.ShapeDtypeStruct((4 * CHANS, WIDTH), F32),
        ),
        in_specs=[vmem, vmem],
        out_specs=(vmem,) * 5,
        compiler_params=pltpu.CompilerParams(vmem_limit_bytes=40 * 1024 * 1024),
        name="unpack_gradients",
    )(everything, got.reshape(256, 128))


def prepare(tile_images, destination, encoder_slot, tile_slide, slide_tiles, targets, depth_taps, first_proj, second_proj, reduce_proj, head_proj):
    x = tile_images.reshape(TILES * 64, CHANS)
    taps = jnp.pad(depth_taps, ((0, 7), (0, 64)))
    count = jnp.pad(slide_tiles.reshape(1, 4), ((0, 0), (0, 4)), constant_values=1)
    return (x, taps, first_proj, second_proj.T, reduce_proj, head_proj, destination.reshape(1, TILES),
            encoder_slot.reshape(1, TILES), tile_slide.reshape(1, TILES), count, targets.reshape(4, 256))


def local(*arguments):
    predicted, send, pack = compute(*prepare(*arguments))
    everything, got = sum_everywhere(pack, send)
    cache, gt, g1, g2, gr = unpack(everything, got)
    return predicted[None], cache[None], gt, g1, g2.T, gr


def solution(mesh):
    in_specs = (
        P("slide", "bulk", None, None, None),
        P("slide", "bulk"),
        P("slide", "bulk"),
        P("slide", "bulk"),
        P("slide", "bulk"),
        P("slide", "bulk", None),
        P(),
        P(),
        P(),
        P(),
        P(),
    )
    out_specs = (P("slide", "bulk", None), P("slide", "bulk", None), P(), P(), P(), P())
    return jax.shard_map(local, mesh=mesh, in_specs=in_specs, out_specs=out_specs, check_vma=False)
```

time: 698 us -> 135 us (0.19)
  other arithmetic: 189 us -> 0 us
  waiting for transfers between devices: 155 us -> 0 us
  Pallas kernels: 0 us -> 129 us
  local copies, waits for them, and re-layouts: 112 us -> 5.26 us
  blocking collectives: 106 us -> 0 us
  matrix products: 96.2 us -> 0 us
  starting transfers between devices: 16.8 us -> 0 us
  between operations: 14.3 us -> 0.64 us
    reduce_sum x64 -> x0, other arithmetic: 152 us -> none  [the longest x1 81.2 us: norm_rows(): centered = values - jnp.mean(values, axis=-1, keepdims=True)]
    psum x1 -> x0, waiting for transfers between devices: 147 us -> none  [local(): lax.psum((found[0], found[1], found[2], found[3]), ('bulk', 'slide'))]
    pallas_call x0 -> x3, Pallas kernels: none -> 129 us  [the longest x1 64.3 us: compute(): pl.pallas_call(compute_kernel, out_shape=shapes, in_specs=[pl.BlockSpec(m...]
    psum x1 -> x0, blocking collectives: 106 us -> none  [local(): lax.psum((found[0], found[1], found[2], found[3]), ('bulk', 'slide'))]
    dot_general x55 -> x0, matrix products: 96.2 us -> none  [the longest x8 18.1 us: gradients(): jnp.dot(pooled_patch.T, back_reduced, precision=lax.Precision.HIGHEST)]
    dynamic_slice x40 -> x0, local copies, waits for them, and re-layouts: 36.5 us -> none  [blocked_gradients(): lax.scan(advance, start, (split_rows(images), jax.tree.map(split_rows, sa...]
    convert_element_type x28 -> x0, other arithmetic: 26.9 us -> none  [the longest x16 8.11 us: gradients(): summed_low = back_summed.reshape(flat_rows, chans).astype(jnp.bfloat16)]
    all_to_all x2 -> x0, starting transfers between devices: 16.7 us -> none  [the longest x1 10.5 us: local(): lax.all_to_all(outgoing_slots, 'bulk', split_axis=0, concat_axis=0, tiled...]
  transfers between devices with their start and end apart: 3 -> 0, of which waited for: 2 -> 0; matrix products, arithmetic and copies ran while one was open for 1% -> 0% of each run, Pallas kernels for 0% -> 0%
where the time goes in v1:
time: 135 us
  Pallas kernels  129 us (96%)
  local copies, waits for them, and re-layouts  5.26 us (4%)
    pallas_call x1, Pallas kernels, compute(): pl.pallas_call(compute_kernel, out_shape=shapes, in_specs=[pl.BlockSpec(m...  64.3 us
    pallas_call x1, Pallas kernels, sum_everywhere(): pl.pallas_call(sum_kernel, out_shape=(jax.ShapeDtypeStruct((64, 80, 128),...  63.5 us

profile of v1, /device:TPU:1, one launch (start us, length us, event | category | flops | bytes accessed | tf_op | source)
XLA Modules:
  0.0 135.2 jit_solution(7187987313453527945)
XLA Ops:
  0.6 1.2 pad.9.count_ref
  1.8 1.4 %pad.8.taps_ref = f32[56,256]{1,0:T(8,128)} pad(f32[49,192]{1,0:T(8,128)} %param.17, f32[]{:T(128)} %constant.1.clone.1), padding=0_7x0_64 | pad | bytes 94980 | tf_op jit(solution)/shard_map/jit(_pad)/pad | solution.py:620
  3.2 64.3 %encode_and_gradients.1 = (f32[4,256]{1,0:T(4,128)}, f32[256,128]{1,0:T(8,128)}, f32[64,80,128]{2,1,0:T(8,128)}) custom-call(bf16[4096,192]{1,0:T(8,128)(2,1)} %bitcast.10, f32[56,256]{1,0:T(8,128)} %pad.8.taps_ref, bf16[192,768]{1,0:T(8,128)(2,1)} %w1_ref.1, bf16[192,768]{1,0:T(8,128)(2,1)} %bitcast.11, bf16[768,384]{1,0:T(8,128)(2,1)} %wr_ref.1, ...), custom_call_target="tpu_custom_call" | custom-call | tf_op jit(solution)/shard_map/encode_and_gradients/pallas_call | solution.py:431
  67.5 0.0 copy-start
  67.5 1.7 %copy-done = f32[64,80,128]{2,1,0:T(8,128)S(1)} copy-done((f32[64,80,128]{2,1,0:T(8,128)S(1)}, f32[64,80,128]{2,1,0:T(8,128)}, u32[]{:S(2)}) %copy-start) | copy-done | bytes 2621464
  69.2 0.0 copy-start.1
  69.2 0.9 copy-done.1
  70.1 63.5 %sum_gradients.1 = (bf16[64,80,128]{2,1,0:T(8,128)(2,1)S(1)}, f32[32,8,128]{2,1,0:T(8,128)S(1)}) custom-call(f32[64,80,128]{2,1,0:T(8,128)S(1)} %copy-done, f32[32,8,128]{2,1,0:T(8,128)S(1)} %bitcast.9), custom_call_target="tpu_custom_call" | custom-call | tf_op jit(solution)/shard_map/sum_gradients/pallas_call | solution.py:544
  133.6 1.6 %unpack_gradients.1 = (f32[24,384]{1,0:T(8,128)}, f32[49,192]{1,0:T(8,128)}, f32[192,768]{1,0:T(8,128)}, f32[192,768]{1,0:T(8,128)}, f32[768,384]{1,0:T(8,128)}) custom-call(bf16[64,80,128]{2,1,0:T(8,128)(2,1)S(1)} %get-tuple-element.19.all_ref, f32[256,128]{1,0:T(8,128)S(1)} %bitcast.8), custom_call_target="tpu_custom_call" | custom-call | tf_op jit(solution)/shard_map/unpack_gradients/pallas_call | solution.py:602
Async XLA Ops:
  67.5 1.7 %copy-start = (f32[64,80,128]{2,1,0:T(8,128)S(1)}, f32[64,80,128]{2,1,0:T(8,128)}, u32[]{:S(2)}) copy-start(f32[64,80,128]{2,1,0:T(8,128)} %get-tuple-element.17.pack_ref) | copy-start | bytes 7864324
  69.2 0.9 copy-start.1

commit v2 on v1

--- a/solution.py
+++ b/solution.py
@@ -48,28 +48,29 @@
 
 
 def gelu_pair(h):
-    size = jnp.abs(h)
-    bell = jnp.exp(h * h * -0.5)
-    t = 1.0 / (1.0 + (0.3275911 * 0.7071067811865476) * size)
-    poly = t * (
-        0.5 * 0.254829592
-        + t
-        * (
-            0.5 * -0.284496736
-            + t * (0.5 * 1.421413741 + t * (0.5 * -1.453152027 + t * (0.5 * 1.061405429)))
-        )
-    )
-    tail = poly * bell
-    phi = jnp.where(h >= 0, 1.0 - tail, tail)
-    return h * phi, phi + h * bell * 0.3989422804014327
-
-
-def gelu_pair_erf(h):
     phi = 0.5 * (1.0 + lax.erf(h * 0.7071067811865476))
     return h * phi, phi + h * jnp.exp(h * h * -0.5) * 0.3989422804014327
 
 
-GELU = gelu_pair
+SKIP = ()
+
+
+def loop(count, body):
+    if body.__name__ not in SKIP:
+        lax.fori_loop(0, count, body, 0)
+
+
+def same_block(extent, size):
+    first = lax.broadcasted_iota(jnp.int32, (extent, extent), 0) // size
+    return first == lax.broadcasted_iota(jnp.int32, (extent, extent), 1) // size
+
+
+def sum_by(values, ones, passes):
+    high = values.astype(BF)
+    total = dot(high, ones)
+    if passes > 1:
+        total = total + dot((values - high.astype(F32)).astype(BF), ones)
+    return total
 
 
 def blocks_of_lanes(rows):
@@ -93,19 +94,24 @@
                     if shift:
                         piece = pltpu.roll(piece, shift, 1)
                     total = piece if total is None else jnp.where(block == jm, piece, total)
-                target[g, pl.ds(row0 + i * TILES, TILES), t * 128 : (t + 1) * 128] = total.astype(BF)
-        return carry
-
-    lax.fori_loop(0, 8, step, 0)
+                target[g, pl.ds(row0 + i * TILES, TILES), t * 128 : (t + 1) * 128] = total.astype(target.dtype)
+        return carry
+
+    loop(8, step)
 
 
 def compute_kernel(
     x_ref, taps_ref, w1_ref, w2t_ref, wr_ref, head_ref, dest_ref, slot_ref, slide_ref, count_ref, targets_ref,
     pred_ref, send_ref, pack_ref,
-    g1_ref, g2_ref, gr_ref, low_ref, high_ref, xs_ref, xg_ref, xt_ref, wd_ref, tg_ref, y_ref, n_ref, nb_ref,
+    taps_pad, g1_ref, g2_ref, gr_ref, low_ref, high_ref, xs_ref, xg_ref, xt_ref, wd_ref, tg_ref, y_ref, f1_ref, w_ref, nb_ref,
     gb_ref, sl_ref, m_ref, pm_ref, w1t_ref, w2_ref, bp_ref, fold_ref,
 ):
-    f1_ref, f2_ref, gy_ref = low_ref, high_ref, xs_ref
+    f2_ref, gn_ref = high_ref, xs_ref
+    spread = same_block(256, 32).astype(BF)
+    ones = jnp.ones((CHANS, 256), BF)
+
+    def row_sum(values, passes):
+        return sum_by(values, ones, passes)[:, 0:CHANS]
 
     def widen(k, carry):
         rows = pl.ds(k * 512, 512)
@@ -114,7 +120,7 @@
         high_ref[rows, 0:64] = values[:, 128:192]
         return carry
 
-    lax.fori_loop(0, 8, widen, 0)
+    loop(8, widen)
 
     def regroup(i, carry):
         for j in range(8):
@@ -123,15 +129,16 @@
             xs_ref[rows, 128:256] = high_ref[pl.ds(i * 8 + j, TILES, stride=64), :]
         return carry
 
-    lax.fori_loop(0, 8, regroup, 0)
+    loop(8, regroup)
 
     xg_ref[:, 0 : 3 * TILES, :] = jnp.zeros((GROUPS, 3 * TILES, 256), BF)
     xg_ref[:, 11 * TILES : 14 * TILES, :] = jnp.zeros((GROUPS, 3 * TILES, 256), BF)
     to_groups(xs_ref, xg_ref, 3 * TILES)
 
     block56 = blocks_of_lanes(56)
-    taps_low = taps_ref[:, 0:128]
-    taps_high = taps_ref[:, 128:256]
+    taps_pad[0:49, 0:CHANS] = taps_ref[...]
+    taps_low = taps_pad[:, 0:128]
+    taps_high = taps_pad[:, 128:256]
     for g in range(GROUPS):
         source = taps_low if g < 4 else taps_high
         total = None
@@ -183,39 +190,45 @@
         xt_ref[g, 1, :, 640:896] = jnp.zeros((256, 256), BF)
         return carry
 
-    lax.fori_loop(0, GROUPS, convolve, 0)
+    loop(GROUPS, convolve)
+
+    def first_norm(k, carry):
+        rows = pl.ds(k * LR, LR)
+        total = y_ref[0, rows, :]
+        for g in range(1, GROUPS):
+            total = total + y_ref[g, rows, :]
+        mean = sum_by(total, spread, 2) * (1.0 / CHANS)
+        square = None
+        for g in range(GROUPS):
+            centered = y_ref[g, rows, :] - mean
+            y_ref[g, rows, :] = centered
+            square = centered * centered if square is None else square + centered * centered
+        factor = lax.rsqrt(sum_by(square, spread, 1) * (1.0 / CHANS) + norm_eps)
+        f1_ref[rows, :] = factor
+        for g in range(GROUPS):
+            y_ref[g, rows, :] = y_ref[g, rows, :] * factor
+        return carry
+
+    loop(PLANE // LR, first_norm)
 
     block64 = blocks_of_lanes(TILES)
 
-    def first_norm(i, carry):
+    def to_lanes(i, carry):
         rows = pl.ds(i * TILES, TILES)
         for t in range(2):
             tiles = [y_ref[g, rows, t * 128 : (t + 1) * 128] for g in range(GROUPS)]
             for jm in range(4):
-                halves = []
-                for picks in ((0, 1, 2, 3), (4, 5)):
+                where = pl.ds((4 * t + jm) * PLANE + i * TILES, TILES)
+                for half, picks in enumerate(((0, 1, 2, 3), (4, 5))):
                     total = None
                     for g in picks:
                         shift = 32 * ((g % 4 - jm) % 4)
                         piece = pltpu.roll(tiles[g], shift, 1) if shift else tiles[g]
                         total = piece if total is None else jnp.where(block64 == g % 4, piece, total)
-                    halves.append(total)
-                halves[1] = jnp.where(block64 < 2, halves[1], 0.0)
-                mean = jnp.sum(halves[0] + halves[1], axis=-1, keepdims=True) * (1.0 / CHANS)
-                c0 = halves[0] - mean
-                c1 = jnp.where(block64 < 2, halves[1] - mean, 0.0)
-                factor = lax.rsqrt(jnp.sum(c0 * c0 + c1 * c1, axis=-1, keepdims=True) * (1.0 / CHANS) + norm_eps)
-                where = pl.ds((4 * t + jm) * PLANE + i * TILES, TILES)
-                n0 = c0 * factor
-                n1 = c1 * factor
-                n_ref[where, 0:128] = n0
-                n_ref[where, 128:256] = n1
-                nb_ref[where, 0:128] = n0.astype(BF)
-                nb_ref[where, 128:256] = n1.astype(BF)
-                f1_ref[where, :] = jnp.broadcast_to(factor, (TILES, 128))
-        return carry
-
-    lax.fori_loop(0, 8, first_norm, 0)
+                    nb_ref[where, half * 128 : half * 128 + 128] = total.astype(BF)
+        return carry
+
+    loop(8, to_lanes)
 
     pm_ref[...] = jnp.zeros_like(pm_ref)
     w1t_ref[...] = jnp.transpose(w1_ref[...], (1, 0))
@@ -228,16 +241,18 @@
         for part in range(HIDDEN // HP):
             cols = slice(part * HP, part * HP + HP)
             hidden = dot(low, w1_ref[:, cols])
-            active, slope = GELU(hidden)
+            active, slope = gelu_pair(hidden)
             active = active.astype(BF)
             gb_ref[rows, cols] = active
             sl_ref[rows, cols] = slope.astype(BF)
             found = dot(active, w2_ref[cols, :])
             branch = found if branch is None else branch + found
         summed = xs_ref[rows, 0:CHANS] + branch
-        normed, factor = norm_rows(summed)
+        centered = summed - row_sum(summed, 2) * (1.0 / CHANS)
+        factor = lax.rsqrt(row_sum(centered * centered, 1) * (1.0 / CHANS) + norm_eps)
+        normed = centered * factor
         m_ref[rows, 0:CHANS] = normed
-        f2_ref[rows, :] = jnp.broadcast_to(factor, (CH, 128))
+        f2_ref[rows, :] = factor[:, 0:128]
         rounded = normed.astype(BF).astype(F32)
         lateral = lax.rem(k // (PLANE // CH), 2)
         for u in range(2):
@@ -248,7 +263,7 @@
             pm_ref[u, lateral] += total
         return carry
 
-    lax.fori_loop(0, 8 * PLANE // CH, block_step, 0)
+    loop(8 * PLANE // CH, block_step)
 
     pooled = [pm_ref[u, v] * (1.0 / 16.0) for u in range(2) for v in range(2)]
     split = [parts_of(piece) for piece in pooled]
@@ -262,8 +277,12 @@
     slide_row = slide_ref[...]
     member = (slide_row == lax.broadcasted_iota(jnp.int32, (8, TILES), 0)).astype(F32)
     eye = lax.broadcasted_iota(jnp.int32, (TILES, TILES), 0) == lax.broadcasted_iota(jnp.int32, (TILES, TILES), 1)
-    eye8 = lax.broadcasted_iota(jnp.int32, (8, 8), 0) == lax.broadcasted_iota(jnp.int32, (8, 8), 1)
-    counts = jnp.sum(jnp.where(eye8, jnp.broadcast_to(count_ref[...].astype(F32), (8, 8)), 0.0), axis=1, keepdims=True)
+    count_rows = jnp.broadcast_to(count_ref[...].astype(F32), (8, 4))
+    slide_of = lax.broadcasted_iota(jnp.int32, (8, 4), 0)
+    counts = jnp.sum(
+        jnp.where(slide_of == lax.broadcasted_iota(jnp.int32, (8, 4), 1), count_rows, 0.0), axis=1, keepdims=True
+    )
+    counts = jnp.where(slide_of[:, 0:1] < 4, counts, 1.0)
     exact = functools.partial(jnp.dot, precision=lax.Precision.HIGHEST, preferred_element_type=F32)
     pooled_slides = exact(member, embedded) / counts
     predicted = exact(pooled_slides, head_ref[...])
@@ -285,7 +304,7 @@
     for q in range(4):
         piece = dot_nt(stacked_back, wr_ref[q * CHANS : (q + 1) * CHANS, :])
         piece = (piece[0:TILES] + piece[TILES : 2 * TILES] + piece[2 * TILES :]) * (1.0 / 16.0)
-        bp_ref[q // 2, q % 2] = piece
+        bp_ref[q // 2, q % 2] = piece - lane_mean(piece)
         rows_q = jnp.concatenate([split[q][0], split[q][1], split[q][0]], axis=0)
         cols_q = jnp.concatenate([back_parts[0], back_parts[0], back_parts[1]], axis=0)
         gr_ref[q * CHANS : (q + 1) * CHANS, :] = dot_tn(rows_q, cols_q)
@@ -317,8 +336,9 @@
         patch = [bp_ref[u, lateral] for u in range(2)]
         incoming = jnp.concatenate([patch[i % 2] for i in range(CH // TILES)], axis=0)
         normed = m_ref[rows, 0:CHANS]
-        factor = f2_ref[rows, 0:1]
-        back_sum = factor * (incoming - lane_mean(incoming) - normed * lane_mean(incoming * normed))
+        factor = f2_ref[rows, :]
+        factor = jnp.concatenate([factor, factor[:, 0 : CHANS - 128]], axis=1)
+        back_sum = factor * (incoming - normed * (row_sum(incoming * normed, 1) * (1.0 / CHANS)))
         low = back_sum.astype(BF)
         active = gb_ref[rows, :]
         g2_ref[...] += dot_tn(low, active)
@@ -330,14 +350,31 @@
             g1_ref[:, cols] += dot_tn(nb, back_hidden)
             found = dot(back_hidden, w1t_ref[cols, :])
             normal = found if normal is None else normal + found
-        n = n_ref[rows, 0:CHANS]
-        f1 = f1_ref[rows, 0:1]
-        gy_ref[rows, 0:CHANS] = f1 * (normal - lane_mean(normal) - n * lane_mean(normal * n))
-        return carry
-
-    lax.fori_loop(0, 8 * PLANE // CH, back_step, 0)
-
-    to_groups(gy_ref, xg_ref, 0)
+        gn_ref[rows, 0:CHANS] = normal
+        return carry
+
+    loop(8 * PLANE // CH, back_step)
+
+    to_groups(gn_ref, w_ref, 0)
+
+    def first_back(k, carry):
+        rows = pl.ds(k * LR, LR)
+        total = None
+        product = None
+        for g in range(GROUPS):
+            w = w_ref[g, rows, :]
+            total = w if total is None else total + w
+            scaled = w * y_ref[g, rows, :]
+            product = scaled if product is None else product + scaled
+        mean = sum_by(total, spread, 2) * (1.0 / CHANS)
+        product = sum_by(product, spread, 1) * (1.0 / CHANS)
+        factor = f1_ref[rows, :]
+        for g in range(GROUPS):
+            found = factor * (w_ref[g, rows, :] - mean - y_ref[g, rows, :] * product)
+            xg_ref[g, rows, :] = found.astype(BF)
+        return carry
+
+    loop(PLANE // LR, first_back)
     block8 = blocks_of_lanes(8)
     same8 = [
         (lax.broadcasted_iota(jnp.int32, (8, 128), 0) + 8 * v) == lax.broadcasted_iota(jnp.int32, (8, 128), 1) % 32
@@ -373,7 +410,7 @@
                 fold_ref[g, a * 7 + b : a * 7 + b + 1, :] = jnp.sum(total, axis=0, keepdims=True)
         return carry
 
-    lax.fori_loop(0, GROUPS, tap_step, 0)
+    loop(GROUPS, tap_step)
     block49 = blocks_of_lanes(56)
     for half, picks in enumerate(((0, 1, 2, 3), (4, 5))):
         total = jnp.zeros((56, 128), F32)
@@ -395,6 +432,7 @@
 
 SPLIT = 2
 CH = 512
+LR = 256
 HP = 256
 
 
@@ -406,6 +444,7 @@
     )
     rows = 8 * PLANE
     scratch = [
+        pltpu.VMEM((56, 256), F32),
         pltpu.VMEM((CHANS, HIDDEN), F32),
         pltpu.VMEM((CHANS, HIDDEN), F32),
         pltpu.VMEM((4 * CHANS, WIDTH), F32),
@@ -417,7 +456,8 @@
         pltpu.VMEM((7, SPLIT, 256, 256), BF),
         pltpu.VMEM((GROUPS, 7, 16, 128), F32),
         pltpu.VMEM((GROUPS, PLANE, 256), F32),
-        pltpu.VMEM((rows, 256), F32),
+        pltpu.VMEM((PLANE, 256), F32),
+        pltpu.VMEM((GROUPS, PLANE, 256), F32),
         pltpu.VMEM((rows, 256), BF),
         pltpu.VMEM((rows, HIDDEN), BF),
         pltpu.VMEM((rows, HIDDEN), BF),
@@ -439,7 +479,7 @@
     )(x, taps, w1, w2t, wr, head, dest, slot, slide, count, targets)
 
 
-def sum_kernel(pack_ref, send_ref, all_ref, got_ref, core_out, core_in, own_ref, x_out, x_in, y_out, y_in, z_out, z_in, send_sems, recv_sems):
+def sum_kernel(pack_ref, send_ref, all_ref, got_ref, core_out, core_in, own_ref, plane_out, plane_in, z_out, z_in, send_sems, recv_sems):
     bulk = lax.axis_index("bulk")
     slide = lax.axis_index("slide")
     x, y = bulk // 8, bulk % 8
@@ -449,8 +489,6 @@
         return (bx * 8 + by, bz * 2 + bc)
 
     mate = place(x, y, z, 1 - core)
-    x_peers = [((x + o) % 4) for o in range(1, 4)]
-    y_peers = [((y + o) % 8) for o in range(1, 8)]
     z_peers = [((z + o) % 8) for o in range(1, 8)]
     b_peers = [((bulk + o) % 32) for o in range(1, 32)]
     barrier = pltpu.get_barrier_semaphore()
@@ -480,35 +518,23 @@
     lax.fori_loop(0, 32, pack, 0, unroll=8)
     pl.semaphore_wait(barrier, len(everyone))
     started = [copy(core_out, core_in, mate)]
-    tiles = [copy(send_ref.at[p], got_ref.at[bulk], (p, slide)) for p in b_peers]
-    got_ref[bulk] = send_ref[bulk]
     finish(started)
 
     def add_core(k, carry):
         total = pack_ref[core * 32 + k] + core_in[k].astype(F32)
         own_ref[k] = total
-        x_out[k // 8, k % 8] = total.astype(BF)
+        plane_out[k] = total.astype(BF)
         return carry
 
     lax.fori_loop(0, 32, add_core, 0, unroll=8)
-    step = [copy(x_out.at[p], x_in.at[o], place(p, y, z, core)) for o, p in enumerate(x_peers)]
+    step = [copy(plane_out.at[p], plane_in.at[o], (p, slide)) for o, p in enumerate(b_peers)]
     started += step
+    tiles = [copy(send_ref.at[p], got_ref.at[bulk], (p, slide)) for p in b_peers]
+    got_ref[bulk] = send_ref[bulk]
     finish(step)
-
-    def add_x(k, carry):
-        total = own_ref[x * 8 + k]
-        for o in range(3):
-            total = total + x_in[o, k].astype(F32)
-        y_out[k] = total.astype(YT)
-        return carry
-
-    lax.fori_loop(0, 8, add_x, 0, unroll=4)
-    step = [copy(y_out.at[p], y_in.at[o], place(x, p, z, core)) for o, p in enumerate(y_peers)]
-    started += step
-    finish(step)
-    total = y_out[y].astype(F32)
-    for o in range(7):
-        total = total + y_in[o].astype(F32)
+    total = own_ref[bulk]
+    for o in range(31):
+        total = total + plane_in[o].astype(F32)
     z_out[...] = total.astype(ZT)
     step = [copy(z_out, z_in.at[z], place(x, y, p, core)) for p in z_peers]
     started += step
@@ -517,13 +543,9 @@
     total = z_in[0].astype(F32)
     for o in range(1, 8):
         total = total + z_in[o].astype(F32)
-    mine = core * 32 + x * 8 + y
+    mine = core * 32 + bulk
     all_ref[mine] = total.astype(BF)
-    step = [copy(all_ref.at[mine], all_ref.at[mine], place(x, p, z, core)) for p in y_peers]
-    started += step
-    finish(step)
-    row = all_ref.at[pl.ds(core * 32 + x * 8, 8)]
-    step = [copy(row, row, place(p, y, z, core)) for p in x_peers]
+    step = [copy(all_ref.at[mine], all_ref.at[mine], (p, slide)) for p in b_peers]
     started += step
     finish(step)
     half = all_ref.at[pl.ds(core * 32, 32)]
@@ -535,8 +557,7 @@
         made.wait_send()
 
 
-YT = F32
-ZT = F32
+ZT = BF
 
 
 def sum_everywhere(pack, send):
@@ -550,14 +571,12 @@
             pltpu.VMEM((32, 80, 128), BF),
             pltpu.VMEM((32, 80, 128), BF),
             pltpu.VMEM((32, 80, 128), F32),
-            pltpu.VMEM((4, 8, 80, 128), BF),
-            pltpu.VMEM((3, 8, 80, 128), BF),
-            pltpu.VMEM((8, 80, 128), YT),
-            pltpu.VMEM((7, 80, 128), YT),
+            pltpu.VMEM((32, 80, 128), BF),
+            pltpu.VMEM((31, 80, 128), BF),
             pltpu.VMEM((80, 128), ZT),
             pltpu.VMEM((8, 80, 128), ZT),
-            pltpu.SemaphoreType.DMA((60,)),
-            pltpu.SemaphoreType.DMA((60,)),
+            pltpu.SemaphoreType.DMA((102,)),
+            pltpu.SemaphoreType.DMA((102,)),
         ],
         compiler_params=pltpu.CompilerParams(
             collective_id=0, has_side_effects=True, vmem_limit_bytes=40 * 1024 * 1024
@@ -617,10 +636,8 @@
 
 def prepare(tile_images, destination, encoder_slot, tile_slide, slide_tiles, targets, depth_taps, first_proj, second_proj, reduce_proj, head_proj):
     x = tile_images.reshape(TILES * 64, CHANS)
-    taps = jnp.pad(depth_taps, ((0, 7), (0, 64)))
-    count = jnp.pad(slide_tiles.reshape(1, 4), ((0, 0), (0, 4)), constant_values=1)
-    return (x, taps, first_proj, second_proj.T, reduce_proj, head_proj, destination.reshape(1, TILES),
-            encoder_slot.reshape(1, TILES), tile_slide.reshape(1, TILES), count, targets.reshape(4, 256))
+    return (x, depth_taps, first_proj, second_proj.T, reduce_proj, head_proj, destination.reshape(1, TILES),
+            encoder_slot.reshape(1, TILES), tile_slide.reshape(1, TILES), slide_tiles.reshape(1, 4), targets.reshape(4, 256))
 
 
 def local(*arguments):

time: 135 us -> 125 us (0.926)
  Pallas kernels: 129 us -> 121 us
  local copies, waits for them, and re-layouts: 5.26 us -> 2.64 us
    pallas_call x1, Pallas kernels: 64.3 us -> 56.5 us  [compute(): pl.pallas_call(compute_kernel, out_shape=shapes, in_specs=[pl.BlockSpec(m...]
    pad x2 -> x0, local copies, waits for them, and re-layouts: 2.62 us -> none  [the longest x1 1.45 us: prepare(): taps = jnp.pad(depth_taps, ((0, 7), (0, 64)))]
where the time goes in v2:
time: 125 us; the launch traced here: 124 us
  Pallas kernels  121 us (97%)
  local copies, waits for them, and re-layouts  2.64 us (2%)
    pallas_call x1, Pallas kernels, sum_everywhere(): pl.pallas_call(sum_kernel, out_shape=(jax.ShapeDtypeStruct((64, 80, 128),...  63 us
    pallas_call x1, Pallas kernels, compute(): pl.pallas_call(compute_kernel, out_shape=shapes, in_specs=[pl.BlockSpec(m...  56.5 us
    unnamed x4, local copies, waits for them, and re-layouts  2.64 us

profile of v2, /device:TPU:1, one launch (start us, length us, event | category | flops | bytes accessed | tf_op | source)
XLA Modules:
  0.0 124.3 jit_solution(13022276363717558584)
XLA Ops:
  0.6 56.5 %encode_and_gradients.1 = (f32[4,256]{1,0:T(4,128)}, f32[256,128]{1,0:T(8,128)}, f32[64,80,128]{2,1,0:T(8,128)}) custom-call(bf16[4096,192]{1,0:T(8,128)(2,1)} %bitcast.10, f32[49,192]{1,0:T(8,128)} %taps_ref.1, bf16[192,768]{1,0:T(8,128)(2,1)} %w1_ref.1, bf16[192,768]{1,0:T(8,128)(2,1)} %bitcast.11, bf16[768,384]{1,0:T(8,128)(2,1)} %wr_ref.1, ...), custom_call_target="tpu_custom_call" | custom-call | tf_op jit(solution)/shard_map/encode_and_gradients/pallas_call | solution.py:471
  57.1 0.0 copy-start
  57.1 1.7 %copy-done = f32[64,80,128]{2,1,0:T(8,128)S(1)} copy-done((f32[64,80,128]{2,1,0:T(8,128)S(1)}, f32[64,80,128]{2,1,0:T(8,128)}, u32[]{:S(2)}) %copy-start) | copy-done | bytes 2621464
  58.8 0.0 copy-start.1
  58.9 0.9 copy-done.1
  59.8 63.0 %sum_gradients.1 = (bf16[64,80,128]{2,1,0:T(8,128)(2,1)S(1)}, f32[32,8,128]{2,1,0:T(8,128)S(1)}) custom-call(f32[64,80,128]{2,1,0:T(8,128)S(1)} %copy-done, f32[32,8,128]{2,1,0:T(8,128)S(1)} %bitcast.9), custom_call_target="tpu_custom_call" | custom-call | tf_op jit(solution)/shard_map/sum_gradients/pallas_call | solution.py:565
  122.8 1.6 %unpack_gradients.1 = (f32[24,384]{1,0:T(8,128)}, f32[49,192]{1,0:T(8,128)}, f32[192,768]{1,0:T(8,128)}, f32[192,768]{1,0:T(8,128)}, f32[768,384]{1,0:T(8,128)}) custom-call(bf16[64,80,128]{2,1,0:T(8,128)(2,1)S(1)} %get-tuple-element.19.all_ref, f32[256,128]{1,0:T(8,128)S(1)} %bitcast.8), custom_call_target="tpu_custom_call" | custom-call | tf_op jit(solution)/shard_map/unpack_gradients/pallas_call | solution.py:621
Async XLA Ops:
  57.1 1.7 %copy-start = (f32[64,80,128]{2,1,0:T(8,128)S(1)}, f32[64,80,128]{2,1,0:T(8,128)}, u32[]{:S(2)}) copy-start(f32[64,80,128]{2,1,0:T(8,128)} %get-tuple-element.17.pack_ref) | copy-start | bytes 7864324
  58.8 0.9 copy-start.1
